TPU v7x, 32 devices: a whole 2x2x4 slice. The times are simulated.
32 devices in a mesh: grp: 2 (over x), tm: 16 (over z, y, core).
Axes of the slice: x: 2, y: 2, z: 4, core: 2. Of those that a mesh axis runs over, the one named last changes fastest.
Arguments:
- old_start: float32 [32, 69, 8, 128], P(('grp', 'tm')), parts along dimension 0, may hold values from -6 to 6
- weight_in: bfloat16 [621, 256], replicated, may hold values from -0.25 to 0.25
- weight_mid: bfloat16 [2304, 256], replicated, may hold values from -0.125 to 0.125
- weight_out: bfloat16 [69, 2304], replicated, may hold values from -0.125 to 0.125
- tendency: float32 [69, 69], replicated, may hold values from -0.0078125 to 0.0078125, as said below
Outputs:
- new_start: float32 [32, 69, 8, 128], P(('grp', 'tm')), parts along dimension 0
- correction_size: float32 [138], P('grp'), parts along dimension 0
There are 2 independent parts, one for each index of `grp`. A program takes and returns all parts, laid end to end along the dimension named above; an argument that names none is the same for every part. Nothing has to cross between parts.
Inputs may be any that keep to these rules, and one draw needn't show every extreme that they name: `tendency`: entries of the coupling matrix.
All inputs are finite; a program needn't handle non-finite values.
Results may differ from a plain program's by a relative error of at most 0.0023.
Values sent between devices are 32-bit elements; how exact they have to be, the bound alone decides.
A program may use at most 128 MiB of HBM per device.

v0:
```python
import jax
import jax.numpy as jnp
from jax import lax
from jax.sharding import PartitionSpec as P

FINE = 2


DAMPING = 0.995


def entering(x, axis, combine, identity):
    count, here = (lax.axis_size(axis), lax.axis_index(axis))
    everything = jax.tree.map(lambda part: lax.all_gather(part, axis), x)
    start = jax.tree.map(
        lambda part, zero: jnp.broadcast_to(jnp.asarray(zero, part.dtype), part.shape), x, identity
    )

    def step(k, before):
        reached = k < here
        new = combine(before, jax.tree.map(lambda part: part[k], everything))
        return jax.tree.map(lambda a, b: jnp.where(reached, a, b), new, before)

    return lax.fori_loop(0, count, step, start)


def patches(field):
    channels, rows, columns = field.shape
    wrapped = jnp.concatenate([field[:, :, -1:], field, field[:, :, :1]], axis=2)
    zero_row = jnp.zeros((channels, 1, columns + 2), field.dtype)
    padded = jnp.concatenate([zero_row, wrapped, zero_row], axis=1)
    pieces = [
        padded[:, above : above + rows, left : left + columns]
        for above in range(3)
        for left in range(3)
    ]
    return jnp.stack(pieces, axis=0).reshape(9 * channels, rows * columns)


def conv_forward(field, kernel):
    channels, rows, columns = field.shape
    result = lax.dot_general(
        kernel, patches(field), (((0,), (0,)), ((), ())), preferred_element_type=jnp.float32
    )
    return result.reshape(kernel.shape[1], rows, columns)


def conv_back(field, kernel):
    channels, rows, columns = field.shape
    result = jnp.dot(kernel, patches(field), preferred_element_type=jnp.float32)
    return result.reshape(kernel.shape[0], rows, columns)


def propagate(current, weight_in, weight_mid, weight_out):
    for _ in range(FINE):
        hidden_one = jax.nn.silu(conv_forward(current.astype(jnp.bfloat16), weight_in)).astype(
            jnp.bfloat16
        )
        hidden_two = jax.nn.silu(conv_forward(hidden_one, weight_mid)).astype(jnp.bfloat16)
        current = current + conv_back(hidden_two, weight_out)
    return current


def compose(earlier, later):
    product = jnp.dot(later[0], earlier[0], precision=lax.Precision.HIGHEST)
    shifted = jnp.dot(later[0], earlier[1], precision=lax.Precision.HIGHEST) + later[1]
    return (product, shifted)


def per_device(old_start, weight_in, weight_mid, weight_out, tendency):
    current = old_start[0]
    fields, rows, columns = current.shape
    fine_end = propagate(current, weight_in, weight_mid, weight_out)
    matrix = DAMPING * jnp.eye(fields, dtype=jnp.float32) + tendency
    flat_old = current.reshape(fields, rows * columns)
    flat_fine = fine_end.reshape(fields, rows * columns)
    position = lax.axis_index("tm")
    leading = position == 0
    forcing = jnp.where(
        leading, flat_fine, flat_fine - jnp.dot(matrix, flat_old, precision=lax.Precision.HIGHEST)
    )
    element = jnp.where(leading, jnp.zeros_like(matrix), matrix)
    identity = (jnp.eye(fields, dtype=jnp.float32), jnp.zeros_like(forcing))
    prefix_matrix, prefix_sum = entering((element, forcing), "tm", compose, identity)
    updated = jnp.dot(prefix_matrix, flat_old, precision=lax.Precision.HIGHEST) + prefix_sum
    change = updated - flat_old
    squares = jnp.sum(change * change, axis=1)
    totals = lax.psum(squares, "tm")
    counted = lax.axis_size("tm") * rows * columns
    correction_size = jnp.sqrt(totals / counted + 1e-06)
    return (updated.reshape(1, fields, rows, columns), correction_size)


def solution(mesh):
    in_specs = (P(("grp", "tm"), None, None, None), P(), P(), P(), P())
    out_specs = (P(("grp", "tm"), None, None, None), P("grp"))
    return jax.shard_map(
        per_device, mesh=mesh, in_specs=in_specs, out_specs=out_specs, check_vma=False
    )
```

profile of v0, /device:TPU:0, one launch (start us, length us, event | category | flops | bytes accessed | tf_op | source)
XLA Modules:
  0.0 223.7 jit_solution(14466361490813528300)
XLA Ops:
  15.8 2.1 copy-done.9
  17.9 2.6 %copy.26 = f32[1,256,8,128]{3,2,1,0:T(8,128)} copy(f32[1,256,8,128]{1,3,2,0:T(8,128)} %bitcast.311) | data formatting | bytes 2097152 | tf_op jit(solution)/shard_map/reshape | solution.py:45
  20.5 2.3 %fusion.31 = bf16[9,256,8,128]{3,2,1,0:T(8,128)(2,1)} fusion(bf16[9,256,8,128]{3,2,1,0:T(8,128)(2,1)} %copy-done.9, f32[1,256,8,128]{3,2,1,0:T(8,128)} %copy.26), kind=kLoop, calls=%fused_computation.79 | loop fusion | flops 1310720 | bytes 1572864
  27.2 3.8 %fusion.20 = f32[1024,256]{1,0:T(8,128)S(1)} fusion(bf16[2304,256]{1,0:T(8,128)(2,1)S(1)} %copy-done, bf16[288,8,8,128]{3,2,1,0:T(8,128)(2,1)} %bitcast.331), kind=kOutput, calls=%fused_computation.22 | convolution fusion | flops 1207959552 | bytes 6946816 | tf_op jit(solution)/shard_map/dot_general | solution.py:42
  35.0 2.1 copy-done.10
  37.1 2.6 %copy.30 = f32[1,256,8,128]{3,2,1,0:T(8,128)} copy(f32[1,256,8,128]{1,3,2,0:T(8,128)} %bitcast.313) | data formatting | bytes 2097152 | tf_op jit(solution)/shard_map/reshape | solution.py:45
  39.7 2.3 %fusion.32 = bf16[9,256,8,128]{3,2,1,0:T(8,128)(2,1)} fusion(bf16[9,256,8,128]{3,2,1,0:T(8,128)(2,1)} %copy-done.10, f32[1,256,8,128]{3,2,1,0:T(8,128)} %copy.30), kind=kLoop, calls=%fused_computation.80 | loop fusion | flops 1310720 | bytes 1572864
  46.6 3.3 %fusion.17 = f32[1024,69]{0,1:T(8,128)S(1)} fusion(bf16[69,2304]{1,0:T(8,128)(2,1)S(1)} %copy-done.13, bf16[288,8,8,128]{3,2,1,0:T(8,128)(2,1)} %bitcast.332), kind=kOutput, calls=%fused_computation.19 | convolution fusion | flops 325582848 | bytes 5319168 | tf_op jit(solution)/shard_map/dot_general | solution.py:50
  55.0 1.5 multiply_convert_fusion.3
  59.5 2.1 copy-done.11
  61.7 2.6 %copy.34 = f32[1,256,8,128]{3,2,1,0:T(8,128)} copy(f32[1,256,8,128]{1,3,2,0:T(8,128)} %bitcast.315) | data formatting | bytes 2097152 | tf_op jit(solution)/shard_map/reshape | solution.py:45
  64.2 2.3 %fusion.33 = bf16[9,256,8,128]{3,2,1,0:T(8,128)(2,1)} fusion(bf16[9,256,8,128]{3,2,1,0:T(8,128)(2,1)} %copy-done.11, f32[1,256,8,128]{3,2,1,0:T(8,128)} %copy.34), kind=kLoop, calls=%fused_computation.81 | loop fusion | flops 1310720 | bytes 1572864
  66.5 2.2 fusion.88
  72.0 3.8 %fusion.14 = f32[1024,256]{1,0:T(8,128)S(1)} fusion(bf16[2304,256]{1,0:T(8,128)(2,1)S(1)} %copy-done, bf16[288,8,8,128]{3,2,1,0:T(8,128)(2,1)} %bitcast.333), kind=kOutput, calls=%fused_computation.16 | convolution fusion | flops 1207959552 | bytes 6946816 | tf_op jit(solution)/shard_map/dot_general | solution.py:42
  78.1 1.5 multiply_convert_fusion.1
  82.9 2.1 copy-done.12
  85.0 2.6 %copy.38 = f32[1,256,8,128]{3,2,1,0:T(8,128)} copy(f32[1,256,8,128]{1,3,2,0:T(8,128)} %bitcast.317) | data formatting | bytes 2097152 | tf_op jit(solution)/shard_map/reshape | solution.py:45
  87.6 2.3 %fusion.34 = bf16[9,256,8,128]{3,2,1,0:T(8,128)(2,1)} fusion(bf16[9,256,8,128]{3,2,1,0:T(8,128)(2,1)} %copy-done.12, f32[1,256,8,128]{3,2,1,0:T(8,128)} %copy.38), kind=kLoop, calls=%fused_computation.82 | loop fusion | flops 1310720 | bytes 1572864
  89.9 2.2 fusion.84
  95.5 3.3 %fusion.28 = f32[69,1024]{1,0:T(8,128)S(1)} fusion(bf16[69,2304]{1,0:T(8,128)(2,1)} %param.10, bf16[288,8,8,128]{3,2,1,0:T(8,128)(2,1)} %bitcast.334, f32[69,1024]{1,0:T(8,128)S(1)} %bitcast.318, f32[1024,69]{0,1:T(8,128)S(1)} %fusion.17), kind=kOutput, calls=%fused_computation.54 | convolution fusion | flops 325724160 | bytes 5884416 | tf_op jit(solution)/shard_map/dot_general | solution.py:50
  100.0 25.4 %all-gather.2 = f32[16,69,69]{2,1,0:T(8,128)S(1)} all-gather(f32[1,69,69]{2,1,0:T(8,128)S(1)} %select_bitcast_fusion), channel_id=2, replica_groups=mesh['grp'=2,'tm'=16] {'tm'}, dimensions={0}, use_global_device_ids=true | all-gather | bytes 323748 | tf_op jit(solution)/shard_map/all_gather | solution.py:14
  125.4 32.1 %all-gather.6.cloned.1.call-done = f32[16,69,1024]{2,1,0:T(8,128)} async-done(((f32[1,69,1024]{2,1,0:T(8,128)}), f32[16,69,1024]{2,1,0:T(8,128)}) %all-gather.6.cloned.1.call-update) | async-done | bytes 4522000 | tf_op jit(solution)/shard_map/all_gather | solution.py:14
  157.4 26.4 %while.16 = (s32[]{:T(128)}, f32[69,69]{1,0:T(8,128)S(1)}, f32[69,1024]{1,0:T(8,128)S(1)}, s32[]{:T(128)}, f32[16,69,69]{2,1,0:T(8,128)S(1)}, /*index=5*/f32[16,69,1024]{2,1,0:T(8,128)}, s32[]{:T(128)}, s32[]{:T(128)}) while((s32[]{:T(128)}, f32[69,69]{1,0:T(8,128)S(1)}, f32[69,1024]{1,0:T(8,128)S(1)}, s32[]{:T(128)}, ...), condition=%wide.region_1.2_spmd.clone, body=%wide.region_0.1_spmd.clone.sunk | while | flops 62732664 | bytes 1939864 | solution.py:24
  157.5 1.4 fusion.167
  159.1 1.4 fusion.167
  160.8 1.4 fusion.167
  162.4 1.4 fusion.167
  165.7 1.4 fusion.167
  167.4 1.4 fusion.167
  170.7 1.4 fusion.167
  172.3 1.4 fusion.167
  185.1 31.2 %psum.7 = f32[69]{0:T(128)S(1)} all-reduce(f32[69]{0:T(128)S(1)} %get-tuple-element.159), channel_id=1, replica_groups=mesh['grp'=2,'tm'=16] {'tm'}, use_global_device_ids=true, to_apply=%region_3.4 | all-reduce | flops 69 | bytes 552 | tf_op jit(solution)/shard_map/psum | solution.py:88
  (171 shorter events, 59.3 us)
Async XLA Ops:
  7.2 20.1 %copy-start = (bf16[2304,256]{1,0:T(8,128)(2,1)S(1)}, bf16[2304,256]{1,0:T(8,128)(2,1)}, u32[]{:S(2)}) copy-start(bf16[2304,256]{1,0:T(8,128)(2,1)} %param.9) | copy-start | bytes 3538948
  7.2 150.3 %all-gather.6.cloned.1.call-start = ((), (), s32[]{:S(2)}) async-start(), calls=%async_computation | async-start | bytes 5013504 | tf_op jit(solution)/shard_map/all_gather | solution.py:14
  8.4 2.8 %copy-start.14 = (bf16[621,256]{1,0:T(8,128)(2,1)S(1)}, bf16[621,256]{1,0:T(8,128)(2,1)}, u32[]{:S(2)}) copy-start(bf16[621,256]{1,0:T(8,128)(2,1)} %param.8) | copy-start | bytes 953860
  11.8 1.0 copy-start.4
  15.8 2.1 copy-start.9
  31.0 1.0 copy-start.5
  35.0 2.1 copy-start.10
  39.7 7.0 %copy-start.13 = (bf16[69,2304]{1,0:T(8,128)(2,1)S(1)}, bf16[69,2304]{1,0:T(8,128)(2,1)}, u32[]{:S(2)}) copy-start(bf16[69,2304]{1,0:T(8,128)(2,1)} %param.10) | copy-start | bytes 953860
  45.4 4.5 %copy-start.1 = (f32[1,69,8,128]{3,2,1,0:T(8,128)S(1)}, f32[1,69,8,128]{3,2,1,0:T(8,128)}, u32[]{:S(2)}) copy-start(f32[1,69,8,128]{3,2,1,0:T(8,128)} %param.7) | copy-start | bytes 847876
  50.3 1.7 copy-start.15
  52.6 1.0 copy-start.6
  56.7 0.8 copy-start.2
  59.5 2.1 copy-start.11
  75.8 1.0 copy-start.7
  79.8 0.8 copy-start.3
  82.9 2.1 copy-start.12
  94.2 4.6 %copy-start.8 = (f32[69,69]{1,0:T(8,128)S(1)}, f32[69,69]{1,0:T(8,128)}, u32[]{:S(2)}) copy-start(f32[69,69]{1,0:T(8,128)} %param.11) | copy-start | bytes 57136
Sparse Core Ops, SparseCore 0:
  100.1 57.3 all-gather.5
where the time goes:
time: 225 us; the launch traced here: 224 us
  blocking collectives  56.6 us (25%)
  local copies, waits for them, and re-layouts  50.2 us (22%)
  matrix products  42.1 us (19%)
  waiting for transfers between devices  32.1 us (14%)
  other arithmetic  27.3 us (12%)
  between operations  14.5 us (6%)
    all_gather x1, waiting for transfers between devices, entering(): everything = jax.tree.map(lambda part: lax.all_gather(part, axis), x)  32.1 us
    psum x1, blocking collectives, per_device(): totals = lax.psum(squares, 'tm')  31.2 us
    unnamed x70, local copies, waits for them, and re-layouts  29.2 us
    all_gather x1, blocking collectives, entering(): everything = jax.tree.map(lambda part: lax.all_gather(part, axis), x)  25.4 us
    dot_general x16, matrix products, compose(): jnp.dot(later[0], earlier[1], precision=lax.Precision.HIGHEST) + later[1]  21.9 us
    unnamed x20, other arithmetic  19.2 us
    reshape x8, local copies, waits for them, and re-layouts, conv_forward(): return result.reshape(kernel.shape[1], rows, columns)  13.7 us
    dot_general x4, matrix products, conv_forward(): lax.dot_general(kernel, patches(field), (((0,), (0,)), ((), ())), preferr...  8.8 us
  transfers between devices with their start and end apart: 1, of which 1 were waited for; matrix products, arithmetic and copies ran while one was open for 0% of the time, Pallas kernels for 0%

commit v1 on v0

v1 whole, which is shorter than its diff:
```python
import functools

import jax
import jax.numpy as jnp
from jax import lax
from jax.experimental import pallas as pl
from jax.experimental.pallas import tpu as pltpu
from jax.sharding import PartitionSpec as P

FINE = 2
DAMPING = 0.995
MESH = pl.DeviceIdType.MESH
HIGHEST = lax.Precision.HIGHEST
F32 = jnp.float32
BF16 = jnp.bfloat16

FP = 72
FK = 80


def exact(a, b):
    return jnp.dot(a, b, precision=HIGHEST, preferred_element_type=F32)


def silu(x):
    return 0.5 * x * (1.0 + jnp.tanh(0.5 * x))


def coarse_matrix(ten_ref, mat):
    fields = ten_ref.shape[0]
    mat[...] = jnp.zeros_like(mat)
    mat[0:fields, 0:fields] = ten_ref[...]
    across = lax.broadcasted_iota(jnp.int32, (FP, FP), 0)
    down = lax.broadcasted_iota(jnp.int32, (FP, FP), 1)
    return mat[:, 0:FP] + jnp.where(across == down, DAMPING, 0.0).astype(F32)


def network(u_ref, win_ref, wmid_ref, wout_ref, ten_ref, f_ref, cur, mat, wtall, wi, wo, xt, acc, hcat, h2):
    fields = ten_ref.shape[0]
    ch = win_ref.shape[1]
    rows = cur.shape[0]
    lon = cur.shape[2]
    cells = rows * lon
    wtall[0 : 9 * fields] = win_ref[...].astype(F32)
    wtall[9 * fields :] = jnp.zeros((wtall.shape[0] - 9 * fields, ch), F32)
    wi[...] = jnp.zeros_like(wi)
    wo[...] = jnp.zeros_like(wo)
    for a in range(3):
        for b in range(3):
            t = 3 * a + b
            wi[a, b * FK : (b + 1) * FK] = wtall[t * fields : t * fields + FK].astype(BF16)
            wo[a, b * FK : b * FK + fields] = wout_ref[:, t * ch : (t + 1) * ch]
    cur[...] = jnp.zeros_like(cur)
    for r in range(rows):
        cur[r, 0:fields] = u_ref[pl.ds(r, fields, stride=rows), :]
    for pad in (xt, hcat, h2):
        pad[0:lon] = jnp.zeros((lon, pad.shape[1]), BF16)
        pad[lon + cells :] = jnp.zeros((lon, pad.shape[1]), BF16)

    for _ in range(FINE):
        for r in range(rows):
            x = cur[r]
            wide = jnp.concatenate(
                [pltpu.roll(x, 1, 1), x, pltpu.roll(x, lon - 1, 1), jnp.zeros((xt.shape[1] - 3 * FK, lon), F32)], axis=0
            )
            xt[(r + 1) * lon : (r + 2) * lon] = wide.T.astype(BF16)
        acc[...] = sum(
            jnp.dot(xt[a * lon : a * lon + cells], wi[a], preferred_element_type=F32) for a in range(3)
        )
        for r in range(rows):
            h = silu(acc[r * lon : (r + 1) * lon])
            here = slice((r + 1) * lon, (r + 2) * lon)
            hcat[here, 0:ch] = pltpu.roll(h, 1, 0).astype(BF16)
            hcat[here, ch : 2 * ch] = h.astype(BF16)
            hcat[here, 2 * ch : 3 * ch] = pltpu.roll(h, lon - 1, 0).astype(BF16)
        acc[...] = sum(
            jnp.dot(
                hcat[a * lon : a * lon + cells],
                wmid_ref[a * 3 * ch : (a + 1) * 3 * ch],
                preferred_element_type=F32,
            )
            for a in range(3)
        )
        for r in range(rows):
            h2[(r + 1) * lon : (r + 2) * lon] = silu(acc[r * lon : (r + 1) * lon]).astype(BF16)
        y = sum(
            lax.dot_general(
                wo[a], h2[a * lon : a * lon + cells], (((1,), (1,)), ((), ())), preferred_element_type=F32
            )
            for a in range(3)
        )
        for r in range(rows):
            part = y[:, r * lon : (r + 1) * lon]
            cur[r] = (
                cur[r]
                + part[FK : 2 * FK]
                + pltpu.roll(part[0:FK], 1, 1)
                + pltpu.roll(part[2 * FK : 3 * FK], lon - 1, 1)
            )

    matrix = coarse_matrix(ten_ref, mat)
    later = jnp.where(lax.axis_index("tm") == 0, 0.0, 1.0).astype(F32)
    for q in range(rows // 2):
        fine = jnp.concatenate([cur[2 * q, 0:FP], cur[2 * q + 1, 0:FP]], axis=1)
        old = old_quarter(u_ref, q, fields, rows)
        f_ref[q] = fine - later * exact(matrix, old)


def old_quarter(u_ref, q, fields, rows):
    pair = [u_ref[pl.ds(2 * q + k, fields, stride=rows), :] for k in range(2)]
    flat = jnp.concatenate(pair, axis=1)
    return jnp.concatenate([flat, jnp.zeros((FP - fields, flat.shape[1]), F32)], axis=0)


def scan(n, u_ref, f_ref, ten_ref, new_ref, size_ref, mat, old, near, tot, cross, carry_in, carry_out, carry_side,
         give, keep, back, sq, sems_s, sems_r, sq_s, sq_r):
    fields = ten_ref.shape[0]
    rows = u_ref.shape[0] // fields
    me = lax.axis_index("tm")
    core = lax.rem(me, 2)
    side = lax.rem(me // 2, 2)
    block = me // 4
    blocks = n // 4
    mate = me + 1 - 2 * core
    other = me + 2 - 4 * side
    following = lax.rem(me + 4, n)
    previous = lax.rem(me + n - 4, n)

    barrier = pltpu.get_barrier_semaphore()

    @pl.loop(1, n)
    def _(d):
        pl.semaphore_signal(barrier, inc=1, device_id={"tm": lax.rem(me + d, n)}, device_id_type=MESH)

    pl.semaphore_wait(barrier, n - 1)

    def send(src, dst, k, to):
        return pltpu.make_async_remote_copy(
            src_ref=src, dst_ref=dst, send_sem=sems_s.at[k], recv_sem=sems_r.at[k], device_id={"tm": to}, device_id_type=MESH
        )

    first = [send(f_ref.at[2 * (1 - core) + k], near.at[k], k, mate) for k in range(2)]
    for copy in first:
        copy.start()

    a1 = coarse_matrix(ten_ref, mat)
    a2 = exact(a1, a1)
    a3 = exact(a2, a1)
    a4 = exact(a2, a2)
    for q in range(4):
        old[q] = old_quarter(u_ref, q, fields, rows)

    zero = jnp.zeros(near.shape[1:], F32)
    upper = core == 0
    for copy in first:
        copy.wait_recv()

    def early_late(k):
        mine, theirs = f_ref[2 * core + k], near[k]
        return jnp.where(upper, mine, theirs), jnp.where(upper, theirs, mine)

    for k, quarter in ((0, 1 - side), (1, side)):
        early, late = early_late(quarter)
        tot[k] = exact(a1, early) + late
        if k == 0:
            swap = send(tot.at[0], cross.at[0], 2, other)
            swap.start()
    extra = send(tot.at[1], cross.at[1], 3, other)

    @pl.when(side == 0)
    def _():
        extra.start()
        cross[1] = zero

    swap.wait_recv()
    low = jnp.where(side == 0, tot[1], cross[0])
    high = jnp.where(side == 0, cross[0], tot[1])
    plane = exact(a2, low) + high

    pass_on = send(carry_out, carry_in, 4, following)
    get = send(carry_out, carry_in, 4, previous)
    aside = send(carry_in, carry_side, 5, other)

    @pl.when(block == 0)
    def _():
        carry_in[...] = zero
        carry_side[...] = zero
        carry_out[...] = plane

    @pl.when(block > 0)
    def _():
        get.wait_recv()
        aside.start()
        carry_out[...] = exact(a4, carry_in[...]) + plane

    @pl.when(block < blocks - 1)
    def _():
        pass_on.start()

    @pl.when(side == 1)
    def _():
        extra.wait_recv()

    def results(quarter, carry, offset):
        early, _ = early_late(quarter)
        n0 = jnp.where(side == 0, carry, exact(a2, carry) + offset)
        n1 = exact(a1, n0) + early
        return n0, n1

    tasks = []
    for k in range(2):
        if k == 1:

            @pl.when(block > 0)
            def _():
                aside.wait_recv()

        quarter = side if k == 0 else 1 - side
        n0, n1 = results(quarter, carry_in[...] if k == 0 else carry_side[...], cross[k])
        give[k] = jnp.where(upper, n1, n0)
        keep[quarter] = jnp.where(upper, n0, n1)
        copy = send(give.at[k], back.at[k], 6 + k, mate)
        copy.start()
        tasks.append(copy)

    for copy in tasks:
        copy.wait_recv()

    start = me == 0
    total = jnp.zeros((8, FP), F32)
    ones = jnp.ones((8, near.shape[2]), F32)
    for h in range(2):
        for k in range(2):
            own = h == 0
            half = core if own else 1 - core
            quarter = 2 * half + k
            value = keep[k] if own else back[jnp.where(side == k, 0, 1)]
            before = old[quarter]
            value = jnp.where(start, before, value)
            change = value - before
            total = total + lax.dot_general(
                ones, change * change, (((1,), (1,)), ((), ())), precision=HIGHEST, preferred_element_type=F32
            )
            for j in range(2):
                new_ref[pl.ds(2 * quarter + j, fields, stride=rows), :] = value[0:fields, j * 128 : (j + 1) * 128]

    sq[me] = jnp.concatenate([total, jnp.zeros((8, 128 - FP), F32)], axis=1)

    def share(d):
        to = lax.rem(me + d, n)
        return pltpu.make_async_remote_copy(
            src_ref=sq.at[me], dst_ref=sq.at[me], send_sem=sq_s.at[to], recv_sem=sq_r.at[me], device_id={"tm": to},
            device_id_type=MESH,
        )

    def arrive(d):
        of = lax.rem(me + d, n)
        return pltpu.make_async_remote_copy(
            src_ref=sq.at[of], dst_ref=sq.at[of], send_sem=sq_s.at[of], recv_sem=sq_r.at[of], device_id={"tm": of},
            device_id_type=MESH,
        )

    @pl.loop(1, n)
    def _(d):
        share(d).start()

    @pl.loop(1, n)
    def _(d):
        arrive(d).wait_recv()

    everyone = jnp.sum(sq[...], axis=0)
    counted = n * rows * 128
    size_ref[...] = jnp.sqrt(everyone[0:1, 0:fields] / counted + 1e-06)

    @pl.loop(1, n)
    def _(d):
        share(d).wait_send()

    for copy in first + tasks + [swap]:
        copy.wait_send()

    @pl.when(side == 0)
    def _():
        extra.wait_send()

    @pl.when(block > 0)
    def _():
        aside.wait_send()

    @pl.when(block < blocks - 1)
    def _():
        pass_on.wait_send()


def per_device(n, old_start, weight_in, weight_mid, weight_out, tendency):
    _, fields, rows, lon = old_start.shape
    ch = weight_in.shape[1]
    cells = rows * lon
    wide = lon + cells + lon
    flat = old_start.reshape(fields * rows, lon)
    vmem = pl.BlockSpec(memory_space=pltpu.VMEM)
    quarter = (FP, 2 * lon)
    forcing = pl.pallas_call(
        network,
        out_shape=jax.ShapeDtypeStruct((4,) + quarter, F32),
        in_specs=[vmem] * 5,
        out_specs=vmem,
        scratch_shapes=[
            pltpu.VMEM((rows, FK, lon), F32),
            pltpu.VMEM((FP, 128), F32),
            pltpu.VMEM((640, ch), F32),
            pltpu.VMEM((3, 256, ch), BF16),
            pltpu.VMEM((3, 3 * FK, ch), BF16),
            pltpu.VMEM((wide, 256), BF16),
            pltpu.VMEM((cells, ch), F32),
            pltpu.VMEM((wide, 3 * ch), BF16),
            pltpu.VMEM((wide, ch), BF16),
        ],
        compiler_params=pltpu.CompilerParams(vmem_limit_bytes=40 * 2**20),
        name="network",
    )(flat, weight_in, weight_mid, weight_out, tendency)
    new, size = pl.pallas_call(
        functools.partial(scan, n),
        out_shape=(jax.ShapeDtypeStruct((fields * rows, lon), F32), jax.ShapeDtypeStruct((1, fields), F32)),
        in_specs=[vmem] * 3,
        out_specs=(vmem, vmem),
        scratch_shapes=[
            pltpu.VMEM((FP, 128), F32),
            pltpu.VMEM((4,) + quarter, F32),
            pltpu.VMEM((2,) + quarter, F32),
            pltpu.VMEM((2,) + quarter, F32),
            pltpu.VMEM((2,) + quarter, F32),
            pltpu.VMEM(quarter, F32),
            pltpu.VMEM(quarter, F32),
            pltpu.VMEM(quarter, F32),
            pltpu.VMEM((2,) + quarter, F32),
            pltpu.VMEM((2,) + quarter, F32),
            pltpu.VMEM((2,) + quarter, F32),
            pltpu.VMEM((n, 8, 128), F32),
            pltpu.SemaphoreType.DMA((8,)),
            pltpu.SemaphoreType.DMA((8,)),
            pltpu.SemaphoreType.DMA((n,)),
            pltpu.SemaphoreType.DMA((n,)),
        ],
        compiler_params=pltpu.CompilerParams(
            collective_id=0, has_side_effects=True, vmem_limit_bytes=24 * 2**20
        ),
        name="scan",
    )(flat, forcing, tendency)
    return (new.reshape(old_start.shape), size.reshape(fields))


def solution(mesh):
    in_specs = (P(("grp", "tm"), None, None, None), P(), P(), P(), P())
    out_specs = (P(("grp", "tm"), None, None, None), P("grp"))
    return jax.shard_map(
        functools.partial(per_device, mesh.shape["tm"]),
        mesh=mesh, in_specs=in_specs, out_specs=out_specs, check_vma=False,
    )
```

time: 225 us -> 48.2 us (0.21)
  blocking collectives: 56.6 us -> 0 us
  local copies, waits for them, and re-layouts: 50.2 us -> 6.15 us
  matrix products: 42.1 us -> 0 us
  Pallas kernels: 0 us -> 41.1 us
  waiting for transfers between devices: 32.1 us -> 0 us
  other arithmetic: 27.3 us -> 0 us
  between operations: 14.5 us -> 0.66 us
    dot_general x40 -> x0, matrix products: 42.1 us -> none  [the longest x16 21.9 us: compose(): jnp.dot(later[0], earlier[1], precision=lax.Precision.HIGHEST) + later[1]]
    pallas_call x0 -> x2, Pallas kernels: none -> 41.1 us  [the longest x1 32.2 us: per_device(): pl.pallas_call(functools.partial(scan, n), out_shape=(jax.ShapeDtypeStruc...]
    all_gather x1 -> x0, waiting for transfers between devices: 32.1 us -> none  [entering(): everything = jax.tree.map(lambda part: lax.all_gather(part, axis), x)]
    psum x1 -> x0, blocking collectives: 31.2 us -> none  [per_device(): totals = lax.psum(squares, 'tm')]
    all_gather x1 -> x0, blocking collectives: 25.4 us -> none  [entering(): everything = jax.tree.map(lambda part: lax.all_gather(part, axis), x)]
    unnamed x70 -> x12, local copies, waits for them, and re-layouts: 29.2 us -> 6.15 us
    unnamed x20 -> x0, other arithmetic: 19.2 us -> none
    reshape x9 -> x0, local copies, waits for them, and re-layouts: 14.4 us -> none  [the longest x8 13.7 us: conv_forward(): return result.reshape(kernel.shape[1], rows, columns)]
  transfers between devices with their start and end apart: 1 -> 0, of which waited for: 1 -> 0; matrix products, arithmetic and copies ran while one was open for 0% -> 0% of each run, Pallas kernels for 0% -> 0%
where the time goes in v1:
time: 48.2 us; the launch traced here: 47.9 us
  Pallas kernels  41.1 us (85%)
  local copies, waits for them, and re-layouts  6.15 us (13%)
  between operations  0.66 us (1%)
    pallas_call x1, Pallas kernels, per_device(): pl.pallas_call(functools.partial(scan, n), out_shape=(jax.ShapeDtypeStruc...  32.2 us
    pallas_call x1, Pallas kernels, per_device(): pl.pallas_call(network, out_shape=jax.ShapeDtypeStruct((4,) + quarter, F3...  8.89 us
    unnamed x12, local copies, waits for them, and re-layouts  6.15 us

profile of v1, /device:TPU:0, one launch (start us, length us, event | category | flops | bytes accessed | tf_op | source)
XLA Modules:
  0.0 47.9 jit_solution(1399659015729314847)
XLA Ops:
  0.6 0.0 copy-start
  0.6 1.3 %copy-done = bf16[2304,256]{1,0:T(8,128)(2,1)S(1)} copy-done((bf16[2304,256]{1,0:T(8,128)(2,1)S(1)}, bf16[2304,256]{1,0:T(8,128)(2,1)}, u32[]{:S(2)}) %copy-start) | copy-done | bytes 1179672
  1.9 0.0 copy-start.1
  1.9 1.0 %copy-done.1 = f32[1,69,8,128]{3,2,1,0:T(8,128)S(1)} copy-done((f32[1,69,8,128]{3,2,1,0:T(8,128)S(1)}, f32[1,69,8,128]{3,2,1,0:T(8,128)}, u32[]{:S(2)}) %copy-start.1) | copy-done | bytes 282648
  2.9 0.0 copy-start.2
  2.9 1.0 %copy-done.2 = bf16[69,2304]{1,0:T(8,128)(2,1)S(1)} copy-done((bf16[69,2304]{1,0:T(8,128)(2,1)S(1)}, bf16[69,2304]{1,0:T(8,128)(2,1)}, u32[]{:S(2)}) %copy-start.2) | copy-done | bytes 317976
  3.8 0.0 copy-start.3
  3.8 1.0 %copy-done.3 = bf16[621,256]{1,0:T(8,128)(2,1)S(1)} copy-done((bf16[621,256]{1,0:T(8,128)(2,1)S(1)}, bf16[621,256]{1,0:T(8,128)(2,1)}, u32[]{:S(2)}) %copy-start.3) | copy-done | bytes 317976
  4.8 0.0 copy-start.4
  4.8 0.8 %copy-done.4 = f32[69,69]{1,0:T(8,128)S(1)} copy-done((f32[69,69]{1,0:T(8,128)S(1)}, f32[69,69]{1,0:T(8,128)}, u32[]{:S(2)}) %copy-start.4) | copy-done | bytes 19068
  5.6 8.9 %network.1.f_ref = f32[4,72,256]{2,1,0:T(8,128)S(1)} custom-call(f32[552,128]{1,0:T(8,128)S(1)} %bitcast.3, bf16[621,256]{1,0:T(8,128)(2,1)S(1)} %copy-done.3, bf16[2304,256]{1,0:T(8,128)(2,1)S(1)} %copy-done, bf16[69,2304]{1,0:T(8,128)(2,1)S(1)} %copy-done.2, f32[69,69]{1,0:T(8,128)S(1)} %copy-done.4), custom_call_target="tpu_custom_call" | custom-call | tf_op jit(solution)/shard_map/network/pallas_call | solution.py:303
  14.5 32.2 %scan.1 = (f32[552,128]{1,0:T(8,128)S(1)}, f32[1,69]{1,0:T(1,128)S(1)}) custom-call(f32[552,128]{1,0:T(8,128)S(1)} %bitcast.4, f32[4,72,256]{2,1,0:T(8,128)S(1)} %network.1.f_ref, f32[69,69]{1,0:T(8,128)S(1)} %copy-done.4), custom_call_target="tpu_custom_call" | custom-call | tf_op jit(solution)/shard_map/scan/pallas_call | solution.py:322
  46.7 0.7 %copy.9 = f32[1,69,8,128]{3,2,1,0:T(8,128)} copy(f32[1,69,8,128]{3,2,1,0:T(8,128)S(1)} %bitcast.5) | data formatting | bytes 565248
  47.4 0.5 %copy.10 = f32[69]{0:T(128)} copy(f32[69]{0:T(128)S(1)} %bitcast.6) | data formatting | bytes 552
Async XLA Ops:
  0.6 1.3 %copy-start = (bf16[2304,256]{1,0:T(8,128)(2,1)S(1)}, bf16[2304,256]{1,0:T(8,128)(2,1)}, u32[]{:S(2)}) copy-start(bf16[2304,256]{1,0:T(8,128)(2,1)} %wmid_ref.1) | copy-start | bytes 3538948
  1.9 1.0 %copy-start.1 = (f32[1,69,8,128]{3,2,1,0:T(8,128)S(1)}, f32[1,69,8,128]{3,2,1,0:T(8,128)}, u32[]{:S(2)}) copy-start(f32[1,69,8,128]{3,2,1,0:T(8,128)} %param.5) | copy-start | bytes 847876
  2.9 1.0 %copy-start.2 = (bf16[69,2304]{1,0:T(8,128)(2,1)S(1)}, bf16[69,2304]{1,0:T(8,128)(2,1)}, u32[]{:S(2)}) copy-start(bf16[69,2304]{1,0:T(8,128)(2,1)} %wout_ref.1) | copy-start | bytes 953860
  3.8 1.0 %copy-start.3 = (bf16[621,256]{1,0:T(8,128)(2,1)S(1)}, bf16[621,256]{1,0:T(8,128)(2,1)}, u32[]{:S(2)}) copy-start(bf16[621,256]{1,0:T(8,128)(2,1)} %win_ref.1) | copy-start | bytes 953860
  4.8 0.8 %copy-start.4 = (f32[69,69]{1,0:T(8,128)S(1)}, f32[69,69]{1,0:T(8,128)}, u32[]{:S(2)}) copy-start(f32[69,69]{1,0:T(8,128)} %ten_ref.3) | copy-start | bytes 57136

commit v2 on v0

v2 whole, which is shorter than its diff:
```python
import functools

import jax
import jax.numpy as jnp
from jax import lax
from jax.experimental import pallas as pl
from jax.experimental.pallas import tpu as pltpu
from jax.sharding import PartitionSpec as P

FINE = 2
DAMPING = 0.995
MESH = pl.DeviceIdType.MESH
HIGHEST = lax.Precision.HIGHEST
F32 = jnp.float32
BF16 = jnp.bfloat16

FP = 72
FK = 80


def exact(a, b):
    return jnp.dot(a, b, precision=HIGHEST, preferred_element_type=F32)


def silu(x):
    return 0.5 * x * (1.0 + jnp.tanh(0.5 * x))


def coarse_matrix(ten_ref, mat):
    fields = ten_ref.shape[0]
    mat[...] = jnp.zeros_like(mat)
    mat[0:fields, 0:fields] = ten_ref[...]
    across = lax.broadcasted_iota(jnp.int32, (FP, FP), 0)
    down = lax.broadcasted_iota(jnp.int32, (FP, FP), 1)
    return mat[:, 0:FP] + jnp.where(across == down, DAMPING, 0.0).astype(F32)


def program(n, u_hbm, win_hbm, wmid_hbm, wout_hbm, ten_hbm, new_hbm, size_ref,
            u_ref, win_ref, wmid_ref, wout_ref, ten_ref, new_ref,
            cur, mat, wtall, wi, wo, xt, acc, hcat, h2,
            old, old_mate, force, near, pair, gather, carry, ahead, give, keep, back, sq,
            load, store, old_s, old_r, near_s, near_r, pair_s, pair_r, carry_s, carry_r, back_s, back_r, sq_s, sq_r):
    fields = ten_ref.shape[0]
    ch = win_ref.shape[1]
    rows, _, lon = cur.shape
    cells = rows * lon
    half = rows // 2
    chips = n // 2
    me = lax.axis_index("tm")
    core = lax.rem(me, 2)
    chip = me // 2
    mate = me + 1 - 2 * core
    upper = core == 0

    loads = [
        pltpu.make_async_copy(src, dst, load.at[k])
        for k, (src, dst) in enumerate(
            ((win_hbm, win_ref), (u_hbm, u_ref), (wout_hbm, wout_ref), (ten_hbm, ten_ref), (wmid_hbm, wmid_ref))
        )
    ]
    for copy in loads:
        copy.start()
    barrier = pltpu.get_barrier_semaphore()

    @pl.loop(1, n)
    def _(d):
        pl.semaphore_signal(barrier, inc=1, device_id={"tm": lax.rem(me + d, n)}, device_id_type=MESH)

    def send(src, dst, sent, got, to):
        return pltpu.make_async_remote_copy(
            src_ref=src, dst_ref=dst, send_sem=sent, recv_sem=got, device_id={"tm": to}, device_id_type=MESH
        )

    wi[...] = jnp.zeros_like(wi)
    wo[...] = jnp.zeros_like(wo)
    cur[...] = jnp.zeros_like(cur)
    for pad in (xt, hcat, h2):
        pad[0:lon] = jnp.zeros((lon, pad.shape[1]), BF16)
        pad[lon + cells :] = jnp.zeros((lon, pad.shape[1]), BF16)
    wtall[9 * fields :] = jnp.zeros((wtall.shape[0] - 9 * fields, ch), F32)
    loads[0].wait()
    wtall[0 : 9 * fields] = win_ref[...].astype(F32)
    for t in range(9):
        a, b = divmod(t, 3)
        wi[a, b * FK : (b + 1) * FK] = wtall[t * fields : t * fields + FK].astype(BF16)
    loads[1].wait()
    for r in range(rows):
        cur[r, 0:fields] = u_ref[pl.ds(r, fields, stride=rows), :]
        old[r] = cur[r, 0:FP]
    loads[2].wait()
    for t in range(9):
        a, b = divmod(t, 3)
        wo[a, b * FK : b * FK + fields] = wout_ref[:, t * ch : (t + 1) * ch]
    loads[3].wait()
    a1 = coarse_matrix(ten_ref, mat)
    a2 = exact(a1, a1)
    moved = jnp.where(me == 0, 0.0, 1.0).astype(F32)

    for step in range(FINE):
        for r in range(rows):
            x = cur[r]
            wide = jnp.concatenate(
                [pltpu.roll(x, 1, 1), x, pltpu.roll(x, lon - 1, 1), jnp.zeros((xt.shape[1] - 3 * FK, lon), F32)], axis=0
            )
            xt[(r + 1) * lon : (r + 2) * lon] = wide.T.astype(BF16)
        acc[...] = sum(
            jnp.dot(xt[a * lon : a * lon + cells], wi[a], preferred_element_type=F32) for a in range(3)
        )
        for r in range(rows):
            h = silu(acc[r * lon : (r + 1) * lon])
            here = slice((r + 1) * lon, (r + 2) * lon)
            hcat[here, 0:ch] = pltpu.roll(h, 1, 0).astype(BF16)
            hcat[here, ch : 2 * ch] = h.astype(BF16)
            hcat[here, 2 * ch : 3 * ch] = pltpu.roll(h, lon - 1, 0).astype(BF16)
        if step == 0:
            loads[4].wait()
        acc[...] = sum(
            jnp.dot(
                hcat[a * lon : a * lon + cells],
                wmid_ref[a * 3 * ch : (a + 1) * 3 * ch],
                preferred_element_type=F32,
            )
            for a in range(3)
        )
        for r in range(rows):
            h2[(r + 1) * lon : (r + 2) * lon] = silu(acc[r * lon : (r + 1) * lon]).astype(BF16)
        for part in (1 - core, core):
            first = part * half
            y = sum(
                lax.dot_general(
                    wo[a],
                    h2[pl.ds(pl.multiple_of((first + a) * lon, lon), half * lon), :],
                    (((1,), (1,)), ((), ())),
                    preferred_element_type=F32,
                )
                for a in range(3)
            )
            for k in range(half):
                piece = y[:, k * lon : (k + 1) * lon]
                cur[first + k] = (
                    cur[first + k]
                    + piece[FK : 2 * FK]
                    + pltpu.roll(piece[0:FK], 1, 1)
                    + pltpu.roll(piece[2 * FK : 3 * FK], lon - 1, 1)
                )
            if step == FINE - 1:
                before = jnp.concatenate([old[first + k] for k in range(half)], axis=1)
                mapped = moved * exact(a1, before)
                for k in range(half):
                    force[first + k] = cur[first + k, 0:FP] - mapped[:, k * lon : (k + 1) * lon]
                if part is not core:
                    to_mate = send(force.at[pl.ds(first, half)], near, near_s, near_r, mate)
                    to_mate.start()
        if step == 0:
            pl.semaphore_wait(barrier, n - 1)
            olds = send(old.at[pl.ds((1 - core) * half, half)], old_mate, old_s, old_r, mate)
            olds.start()

    mine = core * half
    base = chips // 2 - half // 2
    place = chip - base
    owner = jnp.logical_and(place >= 0, place < half)
    place = jnp.clip(place, 0, half - 1)

    to_mate.wait_recv()
    early = jnp.concatenate([jnp.where(upper, force[mine + k], near[k]) for k in range(half)], axis=1)
    mixed = exact(a1, early)
    gives = [
        send(pair.at[k], gather.at[chip], pair_s.at[k], pair_r.at[chip], 2 * (base + k) + core) for k in range(half)
    ]
    for k in range(half):
        late = jnp.where(upper, near[k], force[mine + k])
        pair[k] = mixed[:, k * lon : (k + 1) * lon] + late

        @pl.when(jnp.logical_and(chip != base + k, chip != chips - 1))
        def _():
            gives[k].start()

    @pl.when(chip == 0)
    def _():
        carry[...] = jnp.zeros_like(carry)

    def onward(g):
        return send(ahead.at[g], carry.at[place], carry_s.at[g], carry_r.at[place], 2 * g + core)

    @pl.when(owner)
    def _():
        gather[chip] = pair[place]
        value = None
        for g in range(chips - 1):

            @pl.when(chip != g)
            def _():
                send(pair.at[0], gather.at[g], pair_s.at[0], pair_r.at[g], 2 * g + core).wait_recv()

            value = gather[g] if g == 0 else exact(a2, value) + gather[g]
            ahead[g + 1] = value

            @pl.when(chip != g + 1)
            def _():
                onward(g + 1).start()

            @pl.when(chip == g + 1)
            def _():
                carry[place] = ahead[g + 1]

    olds.wait_recv()
    squares = jnp.zeros((FP, lon), F32)
    returns = []
    for k in range(half):

        @pl.when(jnp.logical_and(chip != 0, chip != base + k))
        def _():
            send(pair.at[0], carry.at[k], pair_s.at[0], carry_r.at[k], 2 * (base + k) + core).wait_recv()

        arrived = carry[k]
        mine_old, mate_old = old[mine + k], old_mate[k]
        n1 = exact(a1, arrived) + early[:, k * lon : (k + 1) * lon]
        n0 = jnp.where(chip == 0, jnp.where(upper, mine_old, mate_old), arrived)
        give[k] = jnp.where(upper, n1, n0)
        copy = send(give.at[k], back.at[k], back_s.at[k], back_r.at[k], mate)
        copy.start()
        returns.append(copy)
        kept = jnp.where(upper, n0, n1)
        keep[k] = kept
        d0, d1 = kept - mine_old, give[k] - mate_old
        squares = squares + (d0 * d0 + d1 * d1)

    total = lax.dot_general(
        jnp.ones((8, lon), F32), squares, (((1,), (1,)), ((), ())), precision=HIGHEST, preferred_element_type=F32
    )
    sq[me] = jnp.concatenate([total, jnp.zeros((8, lon - FP), F32)], axis=1)

    def share(d):
        to = lax.rem(me + d, n)
        return send(sq.at[me], sq.at[me], sq_s.at[to], sq_r.at[me], to)

    def arrive(d):
        of = lax.rem(me + d, n)
        return send(sq.at[of], sq.at[of], sq_s.at[of], sq_r.at[of], of)

    @pl.loop(1, n)
    def _(d):
        share(d).start()

    for k in range(half):
        new_ref[pl.ds(mine + k, fields, stride=rows), :] = keep[k, 0:fields]
    for k in range(half):
        returns[k].wait_recv()
        new_ref[pl.ds(half - mine + k, fields, stride=rows), :] = back[k, 0:fields]
    out = pltpu.make_async_copy(new_ref, new_hbm, store)
    out.start()

    @pl.loop(1, n)
    def _(d):
        arrive(d).wait_recv()

    everyone = jnp.sum(sq[...], axis=0)
    size_ref[...] = jnp.sqrt(everyone[0:1, 0:fields] / (n * cells) + 1e-06)

    @pl.loop(1, n)
    def _(d):
        share(d).wait_send()

    for copy in [olds, to_mate] + returns:
        copy.wait_send()
    for k in range(half):

        @pl.when(jnp.logical_and(chip != base + k, chip != chips - 1))
        def _():
            gives[k].wait_send()

    @pl.when(owner)
    def _():
        for g in range(1, chips):

            @pl.when(chip != g)
            def _():
                onward(g).wait_send()

    out.wait()


def per_device(n, old_start, weight_in, weight_mid, weight_out, tendency):
    _, fields, rows, lon = old_start.shape
    ch = weight_in.shape[1]
    cells = rows * lon
    half = rows // 2
    wide = lon + cells + lon
    chips = n // 2
    flat = old_start.reshape(fields * rows, lon)
    args = (flat, weight_in, weight_mid, weight_out, tendency)
    hbm = pl.BlockSpec(memory_space=pl.ANY)
    dma = pltpu.SemaphoreType.DMA

    def state(*lead):
        return pltpu.VMEM(lead + (FP, lon), F32)

    new, size = pl.pallas_call(
        functools.partial(program, n),
        out_shape=(jax.ShapeDtypeStruct(flat.shape, F32), jax.ShapeDtypeStruct((1, fields), F32)),
        in_specs=[hbm] * 5,
        out_specs=(hbm, pl.BlockSpec(memory_space=pltpu.VMEM)),
        scratch_shapes=[pltpu.VMEM(a.shape, a.dtype) for a in args]
        + [
            pltpu.VMEM(flat.shape, F32),
            pltpu.VMEM((rows, FK, lon), F32),
            pltpu.VMEM((FP, 128), F32),
            pltpu.VMEM((640, ch), F32),
            pltpu.VMEM((3, 256, ch), BF16),
            pltpu.VMEM((3, 3 * FK, ch), BF16),
            pltpu.VMEM((wide, 256), BF16),
            pltpu.VMEM((cells, ch), F32),
            pltpu.VMEM((wide, 3 * ch), BF16),
            pltpu.VMEM((wide, ch), BF16),
            state(rows),
            state(half),
            state(rows),
            state(half),
            state(half),
            state(chips),
            state(half),
            state(chips),
            state(half),
            state(half),
            state(half),
            pltpu.VMEM((n, 8, 128), F32),
            dma((5,)),
            dma,
            dma,
            dma,
            dma,
            dma,
            dma((half,)),
            dma((chips,)),
            dma((chips,)),
            dma((half,)),
            dma((half,)),
            dma((half,)),
            dma((n,)),
            dma((n,)),
        ],
        compiler_params=pltpu.CompilerParams(
            collective_id=0, has_side_effects=True, vmem_limit_bytes=48 * 2**20
        ),
        name="parareal",
    )(*args)
    return (new.reshape(old_start.shape), size.reshape(fields))


def solution(mesh):
    in_specs = (P(("grp", "tm"), None, None, None), P(), P(), P(), P())
    out_specs = (P(("grp", "tm"), None, None, None), P("grp"))
    return jax.shard_map(
        functools.partial(per_device, mesh.shape["tm"]),
        mesh=mesh, in_specs=in_specs, out_specs=out_specs, check_vma=False,
    )
```

time: 225 us -> 38.6 us (0.17)
  blocking collectives: 56.6 us -> 0 us
  local copies, waits for them, and re-layouts: 50.2 us -> 6.15 us
  matrix products: 42.1 us -> 0 us
  waiting for transfers between devices: 32.1 us -> 0 us
  Pallas kernels: 0 us -> 31.4 us
  other arithmetic: 27.3 us -> 0 us
  between operations: 14.5 us -> 0.65 us
    dot_general x40 -> x0, matrix products: 42.1 us -> none  [the longest x16 21.9 us: compose(): jnp.dot(later[0], earlier[1], precision=lax.Precision.HIGHEST) + later[1]]
    all_gather x1 -> x0, waiting for transfers between devices: 32.1 us -> none  [entering(): everything = jax.tree.map(lambda part: lax.all_gather(part, axis), x)]
    pallas_call x0 -> x1, Pallas kernels: none -> 31.4 us  [per_device(): pl.pallas_call(functools.partial(program, n), out_shape=(jax.ShapeDtypeSt...]
    psum x1 -> x0, blocking collectives: 31.2 us -> none  [per_device(): totals = lax.psum(squares, 'tm')]
    all_gather x1 -> x0, blocking collectives: 25.4 us -> none  [entering(): everything = jax.tree.map(lambda part: lax.all_gather(part, axis), x)]
    unnamed x70 -> x12, local copies, waits for them, and re-layouts: 29.2 us -> 6.15 us
    unnamed x20 -> x0, other arithmetic: 19.2 us -> none
    reshape x9 -> x0, local copies, waits for them, and re-layouts: 14.4 us -> none  [the longest x8 13.7 us: conv_forward(): return result.reshape(kernel.shape[1], rows, columns)]
  transfers between devices with their start and end apart: 1 -> 0, of which waited for: 1 -> 0; matrix products, arithmetic and copies ran while one was open for 0% -> 0% of each run, Pallas kernels for 0% -> 0%
where the time goes in v2:
time: 38.6 us; the launch traced here: 38.2 us
  Pallas kernels  31.4 us (81%)
  local copies, waits for them, and re-layouts  6.15 us (16%)
  between operations  0.65 us (2%)
    pallas_call x1, Pallas kernels, per_device(): pl.pallas_call(functools.partial(program, n), out_shape=(jax.ShapeDtypeSt...  31.4 us
    unnamed x12, local copies, waits for them, and re-layouts  6.15 us

profile of v2, /device:TPU:0, one launch (start us, length us, event | category | flops | bytes accessed | tf_op | source)
XLA Modules:
  0.0 38.2 jit_solution(235263125348791741)
XLA Ops:
  0.6 0.0 copy-start
  0.6 1.3 %copy-done = bf16[2304,256]{1,0:T(8,128)(2,1)S(1)} copy-done((bf16[2304,256]{1,0:T(8,128)(2,1)S(1)}, bf16[2304,256]{1,0:T(8,128)(2,1)}, u32[]{:S(2)}) %copy-start) | copy-done | bytes 1179672
  1.9 0.0 copy-start.1
  1.9 1.0 %copy-done.1 = bf16[69,2304]{1,0:T(8,128)(2,1)S(1)} copy-done((bf16[69,2304]{1,0:T(8,128)(2,1)S(1)}, bf16[69,2304]{1,0:T(8,128)(2,1)}, u32[]{:S(2)}) %copy-start.1) | copy-done | bytes 317976
  2.9 0.0 copy-start.2
  2.9 1.0 %copy-done.2 = bf16[621,256]{1,0:T(8,128)(2,1)S(1)} copy-done((bf16[621,256]{1,0:T(8,128)(2,1)S(1)}, bf16[621,256]{1,0:T(8,128)(2,1)}, u32[]{:S(2)}) %copy-start.2) | copy-done | bytes 317976
  3.8 0.0 copy-start.3
  3.9 1.0 %copy-done.3 = f32[1,69,8,128]{3,2,1,0:T(8,128)S(1)} copy-done((f32[1,69,8,128]{3,2,1,0:T(8,128)S(1)}, f32[1,69,8,128]{3,2,1,0:T(8,128)}, u32[]{:S(2)}) %copy-start.3) | copy-done | bytes 282648
  4.8 0.0 copy-start.4
  4.8 0.8 %copy-done.4 = f32[69,69]{1,0:T(8,128)S(1)} copy-done((f32[69,69]{1,0:T(8,128)S(1)}, f32[69,69]{1,0:T(8,128)}, u32[]{:S(2)}) %copy-start.4) | copy-done | bytes 19068
  5.6 31.4 %parareal.1 = (f32[552,128]{1,0:T(8,128)S(1)}, f32[1,69]{1,0:T(1,128)S(1)}) custom-call(f32[552,128]{1,0:T(8,128)S(1)} %bitcast.4, bf16[621,256]{1,0:T(8,128)(2,1)S(1)} %copy-done.2, bf16[2304,256]{1,0:T(8,128)(2,1)S(1)} %copy-done, bf16[69,2304]{1,0:T(8,128)(2,1)S(1)} %copy-done.1, f32[69,69]{1,0:T(8,128)S(1)} %copy-done.4), custom_call_target="tpu_custom_call" | custom-call | tf_op jit(solution)/shard_map/parareal/pallas_call | solution.py:299
  37.0 0.7 %copy.9 = f32[1,69,8,128]{3,2,1,0:T(8,128)} copy(f32[1,69,8,128]{3,2,1,0:T(8,128)S(1)} %bitcast.3) | data formatting | bytes 565248
  37.7 0.5 %copy.10 = f32[69]{0:T(128)} copy(f32[69]{0:T(128)S(1)} %bitcast.5) | data formatting | bytes 552
Async XLA Ops:
  0.6 1.3 %copy-start = (bf16[2304,256]{1,0:T(8,128)(2,1)S(1)}, bf16[2304,256]{1,0:T(8,128)(2,1)}, u32[]{:S(2)}) copy-start(bf16[2304,256]{1,0:T(8,128)(2,1)} %wmid_hbm.1) | copy-start | bytes 3538948
  1.9 1.0 %copy-start.1 = (bf16[69,2304]{1,0:T(8,128)(2,1)S(1)}, bf16[69,2304]{1,0:T(8,128)(2,1)}, u32[]{:S(2)}) copy-start(bf16[69,2304]{1,0:T(8,128)(2,1)} %wout_hbm.1) | copy-start | bytes 953860
  2.9 1.0 %copy-start.2 = (bf16[621,256]{1,0:T(8,128)(2,1)S(1)}, bf16[621,256]{1,0:T(8,128)(2,1)}, u32[]{:S(2)}) copy-start(bf16[621,256]{1,0:T(8,128)(2,1)} %win_hbm.1) | copy-start | bytes 953860
  3.8 1.0 %copy-start.3 = (f32[1,69,8,128]{3,2,1,0:T(8,128)S(1)}, f32[1,69,8,128]{3,2,1,0:T(8,128)}, u32[]{:S(2)}) copy-start(f32[1,69,8,128]{3,2,1,0:T(8,128)} %param.5) | copy-start | bytes 847876
  4.8 0.8 %copy-start.4 = (f32[69,69]{1,0:T(8,128)S(1)}, f32[69,69]{1,0:T(8,128)}, u32[]{:S(2)}) copy-start(f32[69,69]{1,0:T(8,128)} %ten_hbm.1) | copy-start | bytes 57136

commit v3 on v2

--- a/solution.py
+++ b/solution.py
@@ -33,6 +33,14 @@
     across = lax.broadcasted_iota(jnp.int32, (FP, FP), 0)
     down = lax.broadcasted_iota(jnp.int32, (FP, FP), 1)
     return mat[:, 0:FP] + jnp.where(across == down, DAMPING, 0.0).astype(F32)
+
+
+def each_other(n, act):
+    if n <= 32:
+        for d in range(1, n):
+            act(d)
+    else:
+        pl.loop(1, n)(act)
 
 
 def program(n, u_hbm, win_hbm, wmid_hbm, wout_hbm, ten_hbm, new_hbm, size_ref,
@@ -62,9 +70,10 @@
         copy.start()
     barrier = pltpu.get_barrier_semaphore()
 
-    @pl.loop(1, n)
-    def _(d):
+    def greet(d):
         pl.semaphore_signal(barrier, inc=1, device_id={"tm": lax.rem(me + d, n)}, device_id_type=MESH)
+
+    each_other(n, greet)
 
     def send(src, dst, sent, got, to):
         return pltpu.make_async_remote_copy(
@@ -239,9 +248,7 @@
         of = lax.rem(me + d, n)
         return send(sq.at[of], sq.at[of], sq_s.at[of], sq_r.at[of], of)
 
-    @pl.loop(1, n)
-    def _(d):
-        share(d).start()
+    each_other(n, lambda d: share(d).start())
 
     for k in range(half):
         new_ref[pl.ds(mine + k, fields, stride=rows), :] = keep[k, 0:fields]
@@ -251,16 +258,12 @@
     out = pltpu.make_async_copy(new_ref, new_hbm, store)
     out.start()
 
-    @pl.loop(1, n)
-    def _(d):
-        arrive(d).wait_recv()
+    each_other(n, lambda d: arrive(d).wait_recv())
 
     everyone = jnp.sum(sq[...], axis=0)
     size_ref[...] = jnp.sqrt(everyone[0:1, 0:fields] / (n * cells) + 1e-06)
 
-    @pl.loop(1, n)
-    def _(d):
-        share(d).wait_send()
+    each_other(n, lambda d: share(d).wait_send())
 
     for copy in [olds, to_mate] + returns:
         copy.wait_send()
@@ -341,7 +344,7 @@
             dma((n,)),
         ],
         compiler_params=pltpu.CompilerParams(
-            collective_id=0, has_side_effects=True, vmem_limit_bytes=48 * 2**20
+            collective_id=0, has_side_effects=True, vmem_limit_bytes=63 * 2**20
         ),
         name="parareal",
     )(*args)

time: 38.6 us -> 36 us (0.933)
  local copies, waits for them, and re-layouts: 6.15 us -> 2.87 us
  Pallas kernels: 31.4 us -> 32.3 us
    unnamed x12 -> x2, local copies, waits for them, and re-layouts: 6.15 us -> 2.87 us
    pallas_call x1, Pallas kernels: 31.4 us -> 32.3 us  [per_device(): pl.pallas_call(functools.partial(program, n), out_shape=(jax.ShapeDtypeSt...]
where the time goes in v3:
time: 36 us; the launch traced here: 35.8 us
  Pallas kernels  32.3 us (90%)
  local copies, waits for them, and re-layouts  2.87 us (8%)
  between operations  0.64 us (2%)
    pallas_call x1, Pallas kernels, per_device(): pl.pallas_call(functools.partial(program, n), out_shape=(jax.ShapeDtypeSt...  32.3 us
    unnamed x2, local copies, waits for them, and re-layouts  2.87 us

profile of v3, /device:TPU:0, one launch (start us, length us, event | category | flops | bytes accessed | tf_op | source)
XLA Modules:
  0.0 35.8 jit_solution(2018170326444780204)
XLA Ops:
  0.6 32.3 %parareal.1 = (f32[552,128]{1,0:T(8,128)}, f32[1,69]{1,0:T(1,128)}) custom-call(f32[552,128]{1,0:T(8,128)} %bitcast.4, bf16[621,256]{1,0:T(8,128)(2,1)} %win_hbm.1, bf16[2304,256]{1,0:T(8,128)(2,1)} %wmid_hbm.1, bf16[69,2304]{1,0:T(8,128)(2,1)} %wout_hbm.1, f32[69,69]{1,0:T(8,128)} %ten_hbm.1), custom_call_target="tpu_custom_call" | custom-call | tf_op jit(solution)/shard_map/parareal/pallas_call | solution.py:302
  32.9 1.7 %copy.9 = f32[1,69,8,128]{3,2,1,0:T(8,128)} copy(f32[1,69,8,128]{3,2,1,0:T(8,128)} %bitcast.3) | data formatting | bytes 565248
  34.6 1.2 %copy.10 = f32[69]{0:T(128)} copy(f32[69]{0:T(128)} %bitcast.5) | data formatting | bytes 552

commit v4 on v3

--- a/solution.py
+++ b/solution.py
@@ -16,6 +16,7 @@
 
 FP = 72
 FK = 80
+CHUNK = 256
 
 
 def exact(a, b):
@@ -45,9 +46,9 @@
 
 def program(n, u_hbm, win_hbm, wmid_hbm, wout_hbm, ten_hbm, new_hbm, size_ref,
             u_ref, win_ref, wmid_ref, wout_ref, ten_ref, new_ref,
-            cur, mat, wtall, wi, wo, xt, acc, hcat, h2,
+            cur, mat, wtall, wi, wo, xt, hcat, h2,
             old, old_mate, force, near, pair, gather, carry, ahead, give, keep, back, sq,
-            load, store, old_s, old_r, near_s, near_r, pair_s, pair_r, carry_s, carry_r, back_s, back_r, sq_s, sq_r):
+            prior, priors, lead, leads, prior_s, prior_r, lead_s, lead_r, load, store, old_s, old_r, near_s, near_r, pair_s, pair_r, carry_s, carry_r, back_s, back_r, sq_s, sq_r):
     fields = ten_ref.shape[0]
     ch = win_ref.shape[1]
     rows, _, lon = cur.shape
@@ -79,6 +80,18 @@
         return pltpu.make_async_remote_copy(
             src_ref=src, dst_ref=dst, send_sem=sent, recv_sem=got, device_id={"tm": to}, device_id_type=MESH
         )
+
+    mine = core * half
+    base = chips // 2 - half // 2
+    place = chip - base
+    owner = jnp.logical_and(place >= 0, place < half)
+    place = jnp.clip(place, 0, half - 1)
+
+    def to_owner(src, dst, k, sent, got):
+        return send(src.at[k], dst.at[chip], sent.at[k], got.at[chip], 2 * (base + k) + core)
+
+    def from_chip(dst, g, got):
+        return send(pair.at[0], dst.at[g], pair_s.at[0], got.at[g], 2 * g + core)
 
     wi[...] = jnp.zeros_like(wi)
     wo[...] = jnp.zeros_like(wo)
@@ -112,27 +125,41 @@
                 [pltpu.roll(x, 1, 1), x, pltpu.roll(x, lon - 1, 1), jnp.zeros((xt.shape[1] - 3 * FK, lon), F32)], axis=0
             )
             xt[(r + 1) * lon : (r + 2) * lon] = wide.T.astype(BF16)
-        acc[...] = sum(
-            jnp.dot(xt[a * lon : a * lon + cells], wi[a], preferred_element_type=F32) for a in range(3)
-        )
-        for r in range(rows):
-            h = silu(acc[r * lon : (r + 1) * lon])
-            here = slice((r + 1) * lon, (r + 2) * lon)
-            hcat[here, 0:ch] = pltpu.roll(h, 1, 0).astype(BF16)
-            hcat[here, ch : 2 * ch] = h.astype(BF16)
-            hcat[here, 2 * ch : 3 * ch] = pltpu.roll(h, lon - 1, 0).astype(BF16)
+        for m in range(0, cells, CHUNK):
+            wide = silu(
+                sum(
+                    jnp.dot(xt[m + a * lon : m + a * lon + CHUNK], wi[a], preferred_element_type=F32)
+                    for a in range(3)
+                )
+            )
+            for k in range(0, CHUNK, lon):
+                h = wide[k : k + lon]
+                here = slice(m + k + lon, m + k + 2 * lon)
+                hcat[here, 0:ch] = pltpu.roll(h, 1, 0).astype(BF16)
+                hcat[here, ch : 2 * ch] = h.astype(BF16)
+                hcat[here, 2 * ch : 3 * ch] = pltpu.roll(h, lon - 1, 0).astype(BF16)
         if step == 0:
             loads[4].wait()
-        acc[...] = sum(
-            jnp.dot(
-                hcat[a * lon : a * lon + cells],
-                wmid_ref[a * 3 * ch : (a + 1) * 3 * ch],
-                preferred_element_type=F32,
-            )
-            for a in range(3)
-        )
-        for r in range(rows):
-            h2[(r + 1) * lon : (r + 2) * lon] = silu(acc[r * lon : (r + 1) * lon]).astype(BF16)
+        if step == FINE - 1:
+            olds.wait_recv()
+            for k in range(half):
+                prior[k] = jnp.where(upper, old[mine + k], old_mate[k])
+
+                @pl.when(jnp.logical_and(chip != base + k, chip != 0))
+                def _():
+                    to_owner(prior, priors, k, prior_s, prior_r).start()
+
+        for m in range(0, cells, CHUNK):
+            h2[m + lon : m + lon + CHUNK] = silu(
+                sum(
+                    jnp.dot(
+                        hcat[m + a * lon : m + a * lon + CHUNK],
+                        wmid_ref[a * 3 * ch : (a + 1) * 3 * ch],
+                        preferred_element_type=F32,
+                    )
+                    for a in range(3)
+                )
+            ).astype(BF16)
         for part in (1 - core, core):
             first = part * half
             y = sum(
@@ -165,25 +192,23 @@
             olds = send(old.at[pl.ds((1 - core) * half, half)], old_mate, old_s, old_r, mate)
             olds.start()
 
-    mine = core * half
-    base = chips // 2 - half // 2
-    place = chip - base
-    owner = jnp.logical_and(place >= 0, place < half)
-    place = jnp.clip(place, 0, half - 1)
-
     to_mate.wait_recv()
     early = jnp.concatenate([jnp.where(upper, force[mine + k], near[k]) for k in range(half)], axis=1)
     mixed = exact(a1, early)
-    gives = [
-        send(pair.at[k], gather.at[chip], pair_s.at[k], pair_r.at[chip], 2 * (base + k) + core) for k in range(half)
-    ]
     for k in range(half):
         late = jnp.where(upper, near[k], force[mine + k])
         pair[k] = mixed[:, k * lon : (k + 1) * lon] + late
 
         @pl.when(jnp.logical_and(chip != base + k, chip != chips - 1))
         def _():
-            gives[k].start()
+            to_owner(pair, gather, k, pair_s, pair_r).start()
+
+    for k in range(half):
+        lead[k] = early[:, k * lon : (k + 1) * lon] - jnp.where(upper, old_mate[k], old[mine + k])
+
+        @pl.when(chip != base + k)
+        def _():
+            to_owner(lead, leads, k, lead_s, lead_r).start()
 
     @pl.when(chip == 0)
     def _():
@@ -200,7 +225,7 @@
 
             @pl.when(chip != g)
             def _():
-                send(pair.at[0], gather.at[g], pair_s.at[0], pair_r.at[g], 2 * g + core).wait_recv()
+                from_chip(gather, g, pair_r).wait_recv()
 
             value = gather[g] if g == 0 else exact(a2, value) + gather[g]
             ahead[g + 1] = value
@@ -213,8 +238,40 @@
             def _():
                 carry[place] = ahead[g + 1]
 
-    olds.wait_recv()
-    squares = jnp.zeros((FP, lon), F32)
+    slot = 2 * place + core
+
+    def share(d):
+        to = lax.rem(me + d, n)
+        return send(sq.at[slot], sq.at[slot], sq_s.at[to], sq_r.at[slot], to)
+
+    @pl.when(owner)
+    def _():
+        priors[chip] = prior[place]
+        leads[chip] = lead[place]
+        squares = jnp.zeros((FP, lon), F32)
+        for g in range(chips):
+
+            @pl.when(chip != g)
+            def _():
+                from_chip(leads, g, lead_r).wait_recv()
+
+            change = leads[g]
+            if g > 0:
+
+                @pl.when(chip != g)
+                def _():
+                    from_chip(priors, g, prior_r).wait_recv()
+
+                first_change = ahead[g] - priors[g]
+                squares = squares + first_change * first_change
+                change = change + exact(a1, ahead[g])
+            squares = squares + change * change
+        total = lax.dot_general(
+            jnp.ones((8, lon), F32), squares, (((1,), (1,)), ((), ())), precision=HIGHEST, preferred_element_type=F32
+        )
+        sq[slot] = jnp.concatenate([total, jnp.zeros((8, lon - FP), F32)], axis=1)
+        each_other(n, lambda d: share(d).start())
+
     returns = []
     for k in range(half):
 
@@ -223,32 +280,13 @@
             send(pair.at[0], carry.at[k], pair_s.at[0], carry_r.at[k], 2 * (base + k) + core).wait_recv()
 
         arrived = carry[k]
-        mine_old, mate_old = old[mine + k], old_mate[k]
         n1 = exact(a1, arrived) + early[:, k * lon : (k + 1) * lon]
-        n0 = jnp.where(chip == 0, jnp.where(upper, mine_old, mate_old), arrived)
+        n0 = jnp.where(chip == 0, prior[k], arrived)
         give[k] = jnp.where(upper, n1, n0)
         copy = send(give.at[k], back.at[k], back_s.at[k], back_r.at[k], mate)
         copy.start()
         returns.append(copy)
-        kept = jnp.where(upper, n0, n1)
-        keep[k] = kept
-        d0, d1 = kept - mine_old, give[k] - mate_old
-        squares = squares + (d0 * d0 + d1 * d1)
-
-    total = lax.dot_general(
-        jnp.ones((8, lon), F32), squares, (((1,), (1,)), ((), ())), precision=HIGHEST, preferred_element_type=F32
-    )
-    sq[me] = jnp.concatenate([total, jnp.zeros((8, lon - FP), F32)], axis=1)
-
-    def share(d):
-        to = lax.rem(me + d, n)
-        return send(sq.at[me], sq.at[me], sq_s.at[to], sq_r.at[me], to)
-
-    def arrive(d):
-        of = lax.rem(me + d, n)
-        return send(sq.at[of], sq.at[of], sq_s.at[of], sq_r.at[of], of)
-
-    each_other(n, lambda d: share(d).start())
+        keep[k] = jnp.where(upper, n0, n1)
 
     for k in range(half):
         new_ref[pl.ds(mine + k, fields, stride=rows), :] = keep[k, 0:fields]
@@ -258,12 +296,21 @@
     out = pltpu.make_async_copy(new_ref, new_hbm, store)
     out.start()
 
-    each_other(n, lambda d: arrive(d).wait_recv())
+    for other in range(2 * half):
+        of = 2 * (base + other // 2) + other % 2
+
+        @pl.when(me != of)
+        def _():
+            send(sq.at[other], sq.at[other], sq_s.at[of], sq_r.at[other], of).wait_recv()
+
 
     everyone = jnp.sum(sq[...], axis=0)
     size_ref[...] = jnp.sqrt(everyone[0:1, 0:fields] / (n * cells) + 1e-06)
 
-    each_other(n, lambda d: share(d).wait_send())
+    @pl.when(owner)
+    def _():
+        each_other(n, lambda d: share(d).wait_send())
+
 
     for copy in [olds, to_mate] + returns:
         copy.wait_send()
@@ -271,7 +318,15 @@
 
         @pl.when(jnp.logical_and(chip != base + k, chip != chips - 1))
         def _():
-            gives[k].wait_send()
+            to_owner(pair, gather, k, pair_s, pair_r).wait_send()
+
+        @pl.when(chip != base + k)
+        def _():
+            to_owner(lead, leads, k, lead_s, lead_r).wait_send()
+
+        @pl.when(jnp.logical_and(chip != base + k, chip != 0))
+        def _():
+            to_owner(prior, priors, k, prior_s, prior_r).wait_send()
 
     @pl.when(owner)
     def _():
@@ -313,7 +368,6 @@
             pltpu.VMEM((3, 256, ch), BF16),
             pltpu.VMEM((3, 3 * FK, ch), BF16),
             pltpu.VMEM((wide, 256), BF16),
-            pltpu.VMEM((cells, ch), F32),
             pltpu.VMEM((wide, 3 * ch), BF16),
             pltpu.VMEM((wide, ch), BF16),
             state(rows),
@@ -327,7 +381,15 @@
             state(half),
             state(half),
             state(half),
-            pltpu.VMEM((n, 8, 128), F32),
+            pltpu.VMEM((2 * half, 8, lon), F32),
+            state(half),
+            state(chips),
+            state(half),
+            state(chips),
+            dma((half,)),
+            dma((chips,)),
+            dma((half,)),
+            dma((chips,)),
             dma((5,)),
             dma,
             dma,
@@ -341,7 +403,7 @@
             dma((half,)),
             dma((half,)),
             dma((n,)),
-            dma((n,)),
+            dma((2 * half,)),
         ],
         compiler_params=pltpu.CompilerParams(
             collective_id=0, has_side_effects=True, vmem_limit_bytes=63 * 2**20

time: 36 us -> 30.5 us (0.85)
  Pallas kernels: 32.3 us -> 26.8 us
    pallas_call x1, Pallas kernels: 32.3 us -> 26.8 us  [per_device(): pl.pallas_call(functools.partial(program, n), out_shape=(jax.ShapeDtypeSt...]
where the time goes in v4:
time: 30.5 us; the launch traced here: 30.3 us
  Pallas kernels  26.8 us (88%)
  local copies, waits for them, and re-layouts  2.87 us (9%)
  between operations  0.64 us (2%)
    pallas_call x1, Pallas kernels, per_device(): pl.pallas_call(functools.partial(program, n), out_shape=(jax.ShapeDtypeSt...  26.8 us
    unnamed x2, local copies, waits for them, and re-layouts  2.87 us

profile of v4, /device:TPU:0, one launch (start us, length us, event | category | flops | bytes accessed | tf_op | source)
XLA Modules:
  0.0 30.3 jit_solution(13534635845402017553)
XLA Ops:
  0.6 26.8 %parareal.1 = (f32[552,128]{1,0:T(8,128)}, f32[1,69]{1,0:T(1,128)}) custom-call(f32[552,128]{1,0:T(8,128)} %bitcast.4, bf16[621,256]{1,0:T(8,128)(2,1)} %win_hbm.1, bf16[2304,256]{1,0:T(8,128)(2,1)} %wmid_hbm.1, bf16[69,2304]{1,0:T(8,128)(2,1)} %wout_hbm.1, f32[69,69]{1,0:T(8,128)} %ten_hbm.1), custom_call_target="tpu_custom_call" | custom-call | tf_op jit(solution)/shard_map/parareal/pallas_call | solution.py:357
  27.4 1.7 %copy.9 = f32[1,69,8,128]{3,2,1,0:T(8,128)} copy(f32[1,69,8,128]{3,2,1,0:T(8,128)} %bitcast.3) | data formatting | bytes 565248
  29.1 1.2 %copy.10 = f32[69]{0:T(128)} copy(f32[69]{0:T(128)} %bitcast.5) | data formatting | bytes 552

commit v5 on v4

--- a/solution.py
+++ b/solution.py
@@ -406,7 +406,7 @@
             dma((2 * half,)),
         ],
         compiler_params=pltpu.CompilerParams(
-            collective_id=0, has_side_effects=True, vmem_limit_bytes=63 * 2**20
+            collective_id=0, has_side_effects=True, vmem_limit_bytes=54900 * 2**10
         ),
         name="parareal",
     )(*args)

time: 30.5 us -> 29 us (0.951)
  local copies, waits for them, and re-layouts: 2.87 us -> 1.98 us
  Pallas kernels: 26.8 us -> 26.2 us
    unnamed x2 -> x4, local copies, waits for them, and re-layouts: 2.87 us -> 1.98 us
    pallas_call x1, Pallas kernels: 26.8 us -> 26.2 us  [per_device(): pl.pallas_call(functools.partial(program, n), out_shape=(jax.ShapeDtypeSt...]
where the time goes in v5:
time: 29 us; the launch traced here: 28.8 us
  Pallas kernels  26.2 us (90%)
  local copies, waits for them, and re-layouts  1.98 us (7%)
  between operations  0.65 us (2%)
    pallas_call x1, Pallas kernels, per_device(): pl.pallas_call(functools.partial(program, n), out_shape=(jax.ShapeDtypeSt...  26.2 us
    unnamed x4, local copies, waits for them, and re-layouts  1.98 us

profile of v5, /device:TPU:0, one launch (start us, length us, event | category | flops | bytes accessed | tf_op | source)
XLA Modules:
  0.0 28.8 jit_solution(15677800780386872917)
XLA Ops:
  0.6 0.0 copy-start
  0.6 0.8 %copy-done = f32[69,69]{1,0:T(8,128)S(1)} copy-done((f32[69,69]{1,0:T(8,128)S(1)}, f32[69,69]{1,0:T(8,128)}, u32[]{:S(2)}) %copy-start) | copy-done | bytes 19068
  1.4 26.2 %parareal.1 = (f32[552,128]{1,0:T(8,128)S(1)}, f32[1,69]{1,0:T(1,128)S(1)}) custom-call(f32[552,128]{1,0:T(8,128)} %bitcast.5, bf16[621,256]{1,0:T(8,128)(2,1)} %win_hbm.1, bf16[2304,256]{1,0:T(8,128)(2,1)} %wmid_hbm.1, bf16[69,2304]{1,0:T(8,128)(2,1)} %wout_hbm.1, f32[69,69]{1,0:T(8,128)S(1)} %copy-done), custom_call_target="tpu_custom_call" | custom-call | tf_op jit(solution)/shard_map/parareal/pallas_call | solution.py:357
  27.6 0.7 %copy.9 = f32[1,69,8,128]{3,2,1,0:T(8,128)} copy(f32[1,69,8,128]{3,2,1,0:T(8,128)S(1)} %bitcast.3) | data formatting | bytes 565248
  28.3 0.5 %copy.10 = f32[69]{0:T(128)} copy(f32[69]{0:T(128)S(1)} %bitcast.4) | data formatting | bytes 552
Async XLA Ops:
  0.6 0.8 %copy-start = (f32[69,69]{1,0:T(8,128)S(1)}, f32[69,69]{1,0:T(8,128)}, u32[]{:S(2)}) copy-start(f32[69,69]{1,0:T(8,128)} %ten_hbm.1) | copy-start | bytes 57136

commit v6 on v5

--- a/solution.py
+++ b/solution.py
@@ -44,11 +44,11 @@
         pl.loop(1, n)(act)
 
 
-def program(n, u_hbm, win_hbm, wmid_hbm, wout_hbm, ten_hbm, new_hbm, size_ref,
-            u_ref, win_ref, wmid_ref, wout_ref, ten_ref, new_ref,
+def program(n, u_hbm, win_hbm, wmid_hbm, wout_hbm, ten_hbm, new_ref, size_ref,
+            u_ref, win_ref, wmid_ref, wout_ref, ten_ref,
             cur, mat, wtall, wi, wo, xt, hcat, h2,
             old, old_mate, force, near, pair, gather, carry, ahead, give, keep, back, sq,
-            prior, priors, lead, leads, prior_s, prior_r, lead_s, lead_r, load, store, old_s, old_r, near_s, near_r, pair_s, pair_r, carry_s, carry_r, back_s, back_r, sq_s, sq_r):
+            prior, priors, lead, leads, prior_s, prior_r, lead_s, lead_r, load, old_s, old_r, near_s, near_r, pair_s, pair_r, carry_s, carry_r, back_s, back_r, sq_s, sq_r):
     fields = ten_ref.shape[0]
     ch = win_ref.shape[1]
     rows, _, lon = cur.shape
@@ -293,8 +293,6 @@
     for k in range(half):
         returns[k].wait_recv()
         new_ref[pl.ds(half - mine + k, fields, stride=rows), :] = back[k, 0:fields]
-    out = pltpu.make_async_copy(new_ref, new_hbm, store)
-    out.start()
 
     for other in range(2 * half):
         of = 2 * (base + other // 2) + other % 2
@@ -335,8 +333,6 @@
             @pl.when(chip != g)
             def _():
                 onward(g).wait_send()
-
-    out.wait()
 
 
 def per_device(n, old_start, weight_in, weight_mid, weight_out, tendency):
@@ -358,10 +354,9 @@
         functools.partial(program, n),
         out_shape=(jax.ShapeDtypeStruct(flat.shape, F32), jax.ShapeDtypeStruct((1, fields), F32)),
         in_specs=[hbm] * 5,
-        out_specs=(hbm, pl.BlockSpec(memory_space=pltpu.VMEM)),
+        out_specs=(pl.BlockSpec(memory_space=pltpu.VMEM),) * 2,
         scratch_shapes=[pltpu.VMEM(a.shape, a.dtype) for a in args]
         + [
-            pltpu.VMEM(flat.shape, F32),
             pltpu.VMEM((rows, FK, lon), F32),
             pltpu.VMEM((FP, 128), F32),
             pltpu.VMEM((640, ch), F32),
@@ -395,7 +390,6 @@
             dma,
             dma,
             dma,
-            dma,
             dma((half,)),
             dma((chips,)),
             dma((chips,)),

time: 29 us -> 29.4 us (1.014)
  Pallas kernels: 26.2 us -> 26.6 us
    pallas_call x1, Pallas kernels: 26.2 us -> 26.6 us  [per_device(): pl.pallas_call(functools.partial(program, n), out_shape=(jax.ShapeDtypeSt...]
where the time goes in v6:
time: 29.4 us; the launch traced here: 29.2 us
  Pallas kernels  26.6 us (90%)
  local copies, waits for them, and re-layouts  1.98 us (7%)
  between operations  0.65 us (2%)
    pallas_call x1, Pallas kernels, per_device(): pl.pallas_call(functools.partial(program, n), out_shape=(jax.ShapeDtypeSt...  26.6 us
    unnamed x4, local copies, waits for them, and re-layouts  1.98 us

profile of v6, /device:TPU:0, one launch (start us, length us, event | category | flops | bytes accessed | tf_op | source)
XLA Modules:
  0.0 29.2 jit_solution(8328519398583162985)
XLA Ops:
  0.6 0.0 copy-start
  0.6 0.8 %copy-done = f32[69,69]{1,0:T(8,128)S(1)} copy-done((f32[69,69]{1,0:T(8,128)S(1)}, f32[69,69]{1,0:T(8,128)}, u32[]{:S(2)}) %copy-start) | copy-done | bytes 19068
  1.4 26.6 %parareal.1 = (f32[552,128]{1,0:T(8,128)S(1)}, f32[1,69]{1,0:T(1,128)S(1)}) custom-call(f32[552,128]{1,0:T(8,128)} %bitcast.5, bf16[621,256]{1,0:T(8,128)(2,1)} %win_hbm.1, bf16[2304,256]{1,0:T(8,128)(2,1)} %wmid_hbm.1, bf16[69,2304]{1,0:T(8,128)(2,1)} %wout_hbm.1, f32[69,69]{1,0:T(8,128)S(1)} %copy-done), custom_call_target="tpu_custom_call" | custom-call | tf_op jit(solution)/shard_map/parareal/pallas_call | solution.py:353
  28.0 0.7 %copy.9 = f32[1,69,8,128]{3,2,1,0:T(8,128)} copy(f32[1,69,8,128]{3,2,1,0:T(8,128)S(1)} %bitcast.3) | data formatting | bytes 565248
  28.7 0.5 %copy.10 = f32[69]{0:T(128)} copy(f32[69]{0:T(128)S(1)} %bitcast.4) | data formatting | bytes 552
Async XLA Ops:
  0.6 0.8 %copy-start = (f32[69,69]{1,0:T(8,128)S(1)}, f32[69,69]{1,0:T(8,128)}, u32[]{:S(2)}) copy-start(f32[69,69]{1,0:T(8,128)} %ten_hbm.1) | copy-start | bytes 57136
